TPU v7x, 32 devices: a whole 2x2x4 slice. The times are simulated.
32 devices in a mesh: prow: 8 (over y, x, core), pcol: 4 (over z).
Axes of the slice: x: 2, y: 2, z: 4, core: 2. Of those that a mesh axis runs over, the one named last changes fastest.
Arguments:
- designs: float32 [8192, 64], P('prow'), may hold values from -4 to 4
- length_weights: float32 [64], replicated, may hold values from 0.002 to 0.03
- trailing: float32 [16384, 16384], P('prow', 'pcol'), as said below
Outputs:
- updated_trailing: float32 [16384, 16384], P('prow', 'pcol')
- panel_rows: float32 [16384, 512], P('prow', 'pcol')
- panel_factor: float32 [512, 512], P(None, 'pcol')
Inputs may be any that keep to these rules, and one draw needn't show every extreme that they name: `trailing`: symmetric.
All inputs are finite; a program needn't handle non-finite values.
Results may differ from a plain program's by a relative error of at most 0.0003.
Values sent between devices are 32-bit elements; how exact they have to be, the bound alone decides.
A program may use at most 192 MiB of HBM per device.

v0:
```python
import math

import jax
import jax.numpy as jnp
from jax import lax
from jax.sharding import PartitionSpec as P

PANEL = 512
DESIGNS = 8192


signal_variance = 4.0
nugget_level = 0.1


def broadcast(block, axis, holder):
    block = jnp.where(lax.axis_index(axis) == holder, block, jnp.zeros_like(block))
    return lax.psum(block, axis)


def scaled_pair(row_points, panel_points, length_weights):
    root_weights = jnp.sqrt(length_weights)
    return (row_points * root_weights, panel_points * root_weights)


def kernel_values(scaled_rows, scaled_panel):
    inner_terms = jnp.dot(scaled_rows, scaled_panel.T, precision=lax.Precision.HIGHEST)
    squares_rows = jnp.sum(scaled_rows * scaled_rows, axis=1)[:, None]
    squares_panel = jnp.sum(scaled_panel * scaled_panel, axis=1)[None, :]
    return signal_variance * jnp.exp(-(squares_rows + squares_panel - 2.0 * inner_terms))


def cross_block(row_points, panel_points, length_weights):
    scaled_rows, scaled_panel = scaled_pair(row_points, panel_points, length_weights)
    kernel = kernel_values(scaled_rows, scaled_panel)
    panel_gap = scaled_rows[:, -2][:, None] - scaled_panel[:, -2][None, :]
    trail_gap = scaled_rows[:, -1][:, None] - scaled_panel[:, -1][None, :]
    derivative_rows = -2.0 * kernel * trail_gap * panel_gap
    value_rows = math.sqrt(2.0) * kernel * panel_gap
    stacked = jnp.stack([derivative_rows, value_rows], axis=1)
    return stacked.reshape(2 * row_points.shape[0], panel_points.shape[0])


def diagonal_block(row_points, panel_points, length_weights, offset):
    scaled_rows, scaled_panel = scaled_pair(row_points, panel_points, length_weights)
    kernel = kernel_values(scaled_rows, scaled_panel)
    panel_gap = scaled_rows[:, -2][:, None] - scaled_panel[:, -2][None, :]
    row_iota = lax.broadcasted_iota(jnp.int32, kernel.shape, 0)
    col_iota = lax.broadcasted_iota(jnp.int32, kernel.shape, 1) + offset
    return kernel * (1.0 - 2.0 * panel_gap * panel_gap) + jnp.where(
        row_iota == col_iota, nugget_level, 0.0
    )


def right_solve(factor, matrix):
    return jax.scipy.linalg.solve_triangular(factor, matrix.T, lower=True).T


def body(designs, length_weights, trailing):
    per_device = designs.shape[0]
    grid_rows = lax.axis_size("prow")
    grid_cols = lax.axis_size("pcol")
    col_index = lax.axis_index("pcol")
    first_holder = (DESIGNS - PANEL) // per_device
    gathered = [broadcast(designs, "prow", holder) for holder in range(first_holder, grid_rows)]
    panel_points = jnp.concatenate(gathered, 0)[-PANEL:]
    block_width = PANEL // grid_cols
    column_points = lax.dynamic_slice_in_dim(panel_points, col_index * block_width, block_width, 0)
    column_offset = col_index * block_width
    block = jnp.concatenate(
        [
            diagonal_block(panel_points, column_points, length_weights, column_offset),
            cross_block(designs, column_points, length_weights),
        ],
        0,
    )
    row_iota = lax.broadcasted_iota(jnp.int32, block.shape, 0)
    factor_columns = []
    for column_step in range(grid_cols):
        owner_here = col_index == column_step
        diag_part = block[column_step * block_width : (column_step + 1) * block_width]
        diag_part = jnp.where(owner_here, diag_part, jnp.eye(block_width, dtype=jnp.float32))
        diag_factor = jnp.linalg.cholesky(diag_part)
        candidate = right_solve(diag_factor, block)
        candidate = jnp.where(row_iota < column_step * block_width, 0.0, candidate)
        received = broadcast(candidate, "pcol", column_step)
        factor_columns.append(received)
        own_rows = lax.dynamic_slice_in_dim(received, column_offset, block_width, 0)
        reduced = block - jnp.dot(received, own_rows.T, precision=lax.Precision.HIGHEST)
        block = jnp.where(col_index > column_step, reduced, block)
    full_factor = jnp.concatenate(factor_columns, 1)
    panel_factor = full_factor[:PANEL]
    row_factor = full_factor[PANEL:]
    local_rows = row_factor.shape[0]
    row_share = grid_rows // grid_cols
    updated_pieces = []
    for part_step in range(row_share):
        holder_index = col_index * row_share + part_step
        far_rows = broadcast(row_factor, "prow", holder_index)
        trailing_part = trailing[:, part_step * local_rows : (part_step + 1) * local_rows]
        updated_pieces.append(
            trailing_part - jnp.dot(row_factor, far_rows.T, precision=lax.Precision.HIGHEST)
        )
    updated = jnp.concatenate(updated_pieces, 1)
    rows_shard = lax.dynamic_slice_in_dim(row_factor, col_index * block_width, block_width, 1)
    factor_shard = lax.dynamic_slice_in_dim(panel_factor, col_index * block_width, block_width, 1)
    return (updated, rows_shard, factor_shard)


def solution(mesh):
    in_specs = (P("prow", None), P(), P("prow", "pcol"))
    out_specs = (P("prow", "pcol"), P("prow", "pcol"), P(None, "pcol"))
    return jax.shard_map(body, mesh=mesh, in_specs=in_specs, out_specs=out_specs, check_vma=False)
```

profile of v0, /device:TPU:19, one launch (start us, length us, event | category | flops | bytes accessed | tf_op | source)
XLA Modules:
  0.0 676.6 jit_solution(6112651182915498494)
XLA Ops:
  7.2 0.7 sqrt.4
  7.9 1.7 multiply_reduce_fusion
  9.7 54.9 %all-reduce.8.cloned.1.call-done = f32[1024,64]{0,1:T(8,128)} async-done(((f32[1024,64]{0,1:T(8,128)}), f32[1024,64]{0,1:T(8,128)}) %all-reduce.8.cloned.1.call-update) | async-done | bytes 262160 | tf_op jit(solution)/shard_map/psum | solution.py:18
  64.5 1.0 multiply_reduce_fusion.1
  65.6 0.1 multiply_reduce_fusion.2
  65.7 0.5 fusion.22
  66.2 0.1 copy.22
  66.3 11.7 %cholesky.74 = f32[128,128]{1,0:T(8,128)S(1)} custom-call(f32[128,128]{1,0:T(8,128)S(1)} %fusion.37), custom_call_target="Cholesky" | custom-call | tf_op jit(solution)/shard_map/jit(cholesky)/cholesky | solution.py:83
  78.0 0.6 compare_reduce_fusion.3
  78.7 0.7 fusion.26
  79.4 9.8 %custom-call.8 = f32[1,128,128]{1,2,0:T(8,128)S(1)} custom-call(f32[1,128,128]{2,1,0:T(8,128)S(1)} %fusion.26), custom_call_target="InvertDiagBlocksLowerTriangular" | custom-call | tf_op jit(solution)/shard_map/jit(_solve_triangular)/triangular_solve | solution.py:56
  89.2 1.3 fusion.23
  90.6 0.8 copy.23
  91.4 0.3 copy.24
  91.7 2.3 fusion.6
  94.1 0.3 all-reduce.12.cloned.1.call-start
  94.3 60.6 %all-reduce.10.cloned.1.call-done = f32[2560,128]{0,1:T(8,128)} async-done(((f32[2560,128]{0,1:T(8,128)}), f32[2560,128]{0,1:T(8,128)}) %all-reduce.10.cloned.1.call-update) | async-done | bytes 1310736 | tf_op jit(solution)/shard_map/psum | solution.py:18
  155.0 2.6 fusion.5
  157.7 0.1 copy.26
  157.8 11.7 %cholesky.85 = f32[128,128]{1,0:T(8,128)S(1)} custom-call(f32[128,128]{1,0:T(8,128)S(1)} %fusion.35), custom_call_target="Cholesky" | custom-call | tf_op jit(solution)/shard_map/jit(cholesky)/cholesky | solution.py:83
  169.5 0.6 compare_reduce_fusion.2
  170.2 0.7 fusion.27
  170.8 9.8 %custom-call.9 = f32[1,128,128]{1,2,0:T(8,128)S(1)} custom-call(f32[1,128,128]{2,1,0:T(8,128)S(1)} %fusion.27), custom_call_target="InvertDiagBlocksLowerTriangular" | custom-call | tf_op jit(solution)/shard_map/jit(_solve_triangular)/triangular_solve | solution.py:56
  180.7 2.3 fusion.7
  183.0 0.4 all-reduce.14.cloned.1.call-start
  183.5 59.4 %all-reduce.12.cloned.1.call-done = f32[2560,128]{0,1:T(8,128)} async-done(((f32[2560,128]{0,1:T(8,128)}), f32[2560,128]{0,1:T(8,128)}) %all-reduce.12.cloned.1.call-update) | async-done | bytes 1310736 | tf_op jit(solution)/shard_map/psum | solution.py:18
  242.9 2.7 fusion.4
  245.5 0.1 copy.28
  245.7 11.7 %cholesky.96 = f32[128,128]{1,0:T(8,128)S(1)} custom-call(f32[128,128]{1,0:T(8,128)S(1)} %fusion.33), custom_call_target="Cholesky" | custom-call | tf_op jit(solution)/shard_map/jit(cholesky)/cholesky | solution.py:83
  257.4 0.6 compare_reduce_fusion.1
  258.1 0.7 fusion.28
  258.7 9.8 %custom-call.10 = f32[1,128,128]{1,2,0:T(8,128)S(1)} custom-call(f32[1,128,128]{2,1,0:T(8,128)S(1)} %fusion.28), custom_call_target="InvertDiagBlocksLowerTriangular" | custom-call | tf_op jit(solution)/shard_map/jit(_solve_triangular)/triangular_solve | solution.py:56
  268.5 2.3 fusion.8
  270.9 0.2 all-reduce.16.cloned.1.call-start
  271.2 59.6 %all-reduce.14.cloned.1.call-done = f32[2560,128]{0,1:T(8,128)} async-done(((f32[2560,128]{0,1:T(8,128)}), f32[2560,128]{0,1:T(8,128)}) %all-reduce.14.cloned.1.call-update) | async-done | bytes 1310736 | tf_op jit(solution)/shard_map/psum | solution.py:18
  330.7 2.7 fusion.3
  333.4 0.1 copy.30
  333.5 11.7 %cholesky.107 = f32[128,128]{1,0:T(8,128)S(1)} custom-call(f32[128,128]{1,0:T(8,128)S(1)} %fusion.31), custom_call_target="Cholesky" | custom-call | tf_op jit(solution)/shard_map/jit(cholesky)/cholesky | solution.py:83
  345.3 0.6 compare_reduce_fusion
  345.9 0.7 fusion.29
  346.6 9.8 %custom-call.11 = f32[1,128,128]{1,2,0:T(8,128)S(1)} custom-call(f32[1,128,128]{2,1,0:T(8,128)S(1)} %fusion.29), custom_call_target="InvertDiagBlocksLowerTriangular" | custom-call | tf_op jit(solution)/shard_map/jit(_solve_triangular)/triangular_solve | solution.py:56
  356.4 2.3 fusion.9
  358.8 0.3 all-reduce.18.cloned.1.call-start
  359.1 1.0 copy-done
  360.1 1.2 constant_dynamic-update-slice_fusion.3
  361.2 0.6 copy-done.1
  361.9 1.1 constant_dynamic-update-slice_fusion.2
  363.0 0.6 copy-done.2
  363.7 1.2 constant_dynamic-update-slice_fusion.1
  364.8 53.8 %all-reduce.16.cloned.1.call-done = f32[2560,128]{0,1:T(8,128)} async-done(((f32[2560,128]{0,1:T(8,128)}), f32[2560,128]{0,1:T(8,128)}) %all-reduce.16.cloned.1.call-update) | async-done | bytes 1310736 | tf_op jit(solution)/shard_map/psum | solution.py:18
  418.6 2.5 constant_dynamic-update-slice_fusion
  421.1 8.1 %fusion.48 = (f32[2048,512]{0,1:T(8,128)}, f32[2048,512]{0,1:T(8,128)}, f32[2048,512]{0,1:T(8,128)}) fusion(f32[2560,512]{0,1:T(8,128)} %constant_dynamic-update-slice_fusion, pred[]{:T(512)S(6)} %eq.47, pred[]{:T(512)S(6)} %eq.48), kind=kLoop, calls=%fused_computation.110 | loop fusion | flops 2097152 | bytes 16777218 | tf_op jit(solution)/shard_map/slice | solution.py:93
  429.2 21.8 %fusion.47 = (f32[2048,2048]{1,0:T(8,128)}, f32[2048,2048]{1,0:T(8,128)}) fusion(f32[2048,4096]{1,0:T(8,128)} %param.8), kind=kLoop, calls=%fused_computation.109 | loop fusion | bytes 67108864 | tf_op jit(solution)/shard_map/slice | solution.py:100
  451.0 17.9 %copy.39 = f32[2048,2048]{0,1:T(8,128)} copy(f32[2048,2048]{1,0:T(8,128)} %get-tuple-element.19) | data formatting | bytes 33554432
  468.9 17.7 %copy.40 = f32[2048,2048]{0,1:T(8,128)} copy(f32[2048,2048]{1,0:T(8,128)} %get-tuple-element.20) | data formatting | bytes 33554432
  486.7 1.3 slice.76
  488.0 0.8 copy.34
  488.8 1.3 constant_dynamic-slice_fusion.1
  490.2 1.3 copy.33
  491.5 64.7 %all-reduce.18.cloned.1.call-done = (f32[2048,512]{0,1:T(8,128)}, f32[2048,512]{0,1:T(8,128)}) async-done(((f32[2048,512]{0,1:T(8,128)}, f32[2048,512]{0,1:T(8,128)}), (f32[2048,512]{0,1:T(8,128)}, f32[2048,512]{0,1:T(8,128)})) %all-reduce.18.cloned.1.call-update) | async-done | bytes 8388624 | tf_op jit(solution)/shard_map/psum | solution.py:18
  556.1 31.2 %convolution_subtract_fusion.1 = f32[2048,2048]{0,1:T(8,128)S(1)} fusion(f32[2048,2048]{0,1:T(8,128)} %copy.39, f32[2048,512]{0,1:T(8,128)} %get-tuple-element.12, f32[2560,512]{0,1:T(8,128)} %constant_dynamic-update-slice_fusion), kind=kOutput, calls=%fused_computation.2 | convolution fusion | flops 25773998080 | bytes 41943040 | tf_op jit(solution)/shard_map/dot_general | solution.py:102
  587.4 32.0 %convolution_subtract_fusion = f32[2048,2048]{0,1:T(8,128)} fusion(f32[2048,2048]{0,1:T(8,128)} %copy.40, f32[2048,512]{0,1:T(8,128)S(1)} %copy-done.3, f32[2560,512]{0,1:T(8,128)} %constant_dynamic-update-slice_fusion), kind=kOutput, calls=%fused_computation.1 | convolution fusion | flops 25773998080 | bytes 41943040 | tf_op jit(solution)/shard_map/dot_general | solution.py:102
  619.3 18.9 %pad_maximum_fusion = f32[2048,4096]{0,1:T(8,128)} fusion(f32[2048,2048]{0,1:T(8,128)} %convolution_subtract_fusion, f32[2048,2048]{0,1:T(8,128)S(1)} %convolution_subtract_fusion.1), kind=kLoop, calls=%fused_computation | loop fusion | flops 8388608 | bytes 67108864 | tf_op jit(solution)/shard_map/concatenate | solution.py:104
  638.2 31.1 %copy.32 = f32[2048,4096]{1,0:T(8,128)} copy(f32[2048,4096]{0,1:T(8,128)} %pad_maximum_fusion) | data formatting | bytes 67108864
  (34 shorter events, 0.6 us)
Async XLA Ops:
  7.2 57.4 %all-reduce.8.cloned.1.call-start = ((), (), s32[]{:S(2)}) async-start(), calls=%async_computation | async-start | bytes 524288 | tf_op jit(solution)/shard_map/psum | solution.py:18
  9.6 145.4 %all-reduce.10.cloned.1.call-start = ((), (), s32[]{:S(2)}) async-start(), calls=%async_computation.1 | async-start | bytes 2621440 | tf_op jit(solution)/shard_map/psum | solution.py:18
  94.1 148.8 %all-reduce.12.cloned.1.call-start = ((), (), s32[]{:S(2)}) async-start(), calls=%async_computation.2 | async-start | bytes 2621440 | tf_op jit(solution)/shard_map/psum | solution.py:18
  183.0 147.7 %all-reduce.14.cloned.1.call-start = ((), (), s32[]{:S(2)}) async-start(), calls=%async_computation.3 | async-start | bytes 2621440 | tf_op jit(solution)/shard_map/psum | solution.py:18
  270.9 147.7 %all-reduce.16.cloned.1.call-start = ((), (), s32[]{:S(2)}) async-start(), calls=%async_computation.4 | async-start | bytes 2621440 | tf_op jit(solution)/shard_map/psum | solution.py:18
  358.8 1.3 copy-start
  358.8 197.3 %all-reduce.18.cloned.1.call-start = ((), (), s32[]{:S(2)}) async-start(), calls=%async_computation.5 | async-start | bytes 16777216 | tf_op jit(solution)/shard_map/psum | solution.py:18
  360.1 1.8 copy-start.1
  361.9 1.8 copy-start.2
  556.1 31.2 %copy-start.3 = (f32[2048,512]{0,1:T(8,128)S(1)}, f32[2048,512]{0,1:T(8,128)}, u32[]{:S(2)}) copy-start(f32[2048,512]{0,1:T(8,128)} %get-tuple-element.11) | copy-start | bytes 12582916
Sparse Core Ops, SparseCore 0:
  11.6 52.8 all-reduce.7
  94.2 60.7 all-reduce.9
  183.1 59.6 all-reduce.11
  271.0 59.6 all-reduce.13
  358.9 59.6 all-reduce.15
  429.4 126.7 all-reduce.17
where the time goes:
time: 687 us; the launch traced here: 677 us
  waiting for transfers between devices  353 us (51%)
  other arithmetic  121 us (18%)
  local copies, waits for them, and re-layouts  104 us (15%)
  matrix products  82.3 us (12%)
  between operations  14.9 us (2%)
    psum x6, waiting for transfers between devices, broadcast(): return lax.psum(block, axis)  353 us
    unnamed x16, local copies, waits for them, and re-layouts  74.6 us
    dot_general x2, matrix products, body(): jnp.dot(row_factor, far_rows.T, precision=lax.Precision.HIGHEST)  63.2 us
    another operation x12, other arithmetic, body(): diag_factor = jnp.linalg.cholesky(diag_part)  49.6 us
    another operation x8, other arithmetic, right_solve(): return jax.scipy.linalg.solve_triangular(factor, matrix.T, lower=True).T  41.9 us
    slice x1, local copies, waits for them, and re-layouts, body(): trailing[:, part_step * local_rows:(part_step + 1) * local_rows]  21.8 us
    concatenate x1, other arithmetic, body(): updated = jnp.concatenate(updated_pieces, 1)  18.9 us
  transfers between devices with their start and end apart: 6, of which 6 were waited for; matrix products, arithmetic and copies ran while one was open for 10% of the time, Pallas kernels for 0%

commit v1 on v0

v1 whole, which is shorter than its diff:
```python
import functools
import math

import jax
import jax.numpy as jnp
from jax import lax
from jax.experimental import pallas as pl
from jax.experimental.pallas import tpu as pltpu
from jax.sharding import PartitionSpec as P

PANEL = 512
BLOCK = 128
GROUP = 16
MESH = pl.DeviceIdType.MESH
BF16 = jnp.bfloat16
F32 = jnp.float32
HIGHEST = lax.Precision.HIGHEST

signal_variance = 4.0
nugget_level = 0.1


def split2(x):
    high = x.astype(BF16)
    return high, (x - high.astype(F32)).astype(BF16)


def split3(x):
    high = x.astype(BF16)
    rest = x - high.astype(F32)
    mid = rest.astype(BF16)
    return high, mid, (rest - mid.astype(F32)).astype(BF16)


def dot_tn(a, b, precision=None):
    return lax.dot_general(
        a, b, (((0,), (0,)), ((), ())), precision=precision, preferred_element_type=F32
    )


def dot_nt(a, b):
    return lax.dot_general(a, b, (((1,), (1,)), ((), ())), preferred_element_type=F32)


def gather_kernel(grid_rows, grid_cols, own, panel, cols, send_sem, local_sem, panel_sem, cols_sem):
    me = lax.axis_index("prow")
    col = lax.axis_index("pcol")
    per = own.shape[1]
    panel_width = min(per, PANEL)
    holders = PANEL // panel_width
    share = grid_rows // grid_cols
    barrier = pltpu.get_barrier_semaphore()
    for step in range(1, grid_rows):
        peer = lax.rem(me + step, grid_rows)
        pl.semaphore_signal(barrier, inc=1, device_id=(peer, col), device_id_type=MESH)
    pl.semaphore_wait(barrier, grid_rows - 1)

    pieces = []
    for at in range(holders):
        source = own.at[:, per - panel_width :] if panel_width < per else own
        target = panel.at[:, at * panel_width : (at + 1) * panel_width]
        pieces.append((grid_rows - holders + at, source, target, panel_sem.at[at], at))
    for at in range(share):
        target = cols.at[:, at * per : (at + 1) * per]
        pieces.append((col * share + at, own, target, cols_sem.at[at], holders + at))

    def remote(piece, step):
        _, source, target, sem, at = piece
        peer = lax.rem(me + step, grid_rows)
        return pltpu.make_async_remote_copy(
            src_ref=source,
            dst_ref=target,
            send_sem=send_sem.at[at, step - 1],
            recv_sem=sem,
            device_id=(peer, col),
            device_id_type=MESH,
        )

    for piece in pieces:
        holder, source, target, sem, at = piece

        @pl.when(me == holder)
        def _():
            for step in range(1, grid_rows):
                remote(piece, step).start()
            pltpu.make_async_copy(source, target, local_sem.at[at]).start()

    for piece in pieces:
        holder, source, target, sem, at = piece

        @pl.when(me == holder)
        def _():
            for step in range(1, grid_rows):
                remote(piece, step).wait_send()
            pltpu.make_async_copy(source, target, local_sem.at[at]).wait()

        @pl.when(me != holder)
        def _():
            remote(piece, 1).wait_recv()


def gather_designs(own, grid_rows, grid_cols):
    variables, per = own.shape
    holders = PANEL // min(per, PANEL)
    share = grid_rows // grid_cols
    return pl.pallas_call(
        functools.partial(gather_kernel, grid_rows, grid_cols),
        out_shape=(
            jax.ShapeDtypeStruct((variables, PANEL), F32),
            jax.ShapeDtypeStruct((variables, per * share), F32),
        ),
        in_specs=[pl.BlockSpec(memory_space=pltpu.VMEM)],
        out_specs=(pl.BlockSpec(memory_space=pltpu.VMEM), pl.BlockSpec(memory_space=pltpu.VMEM)),
        scratch_shapes=[
            pltpu.SemaphoreType.DMA((holders + share, grid_rows - 1)),
            pltpu.SemaphoreType.DMA((holders + share,)),
            pltpu.SemaphoreType.DMA((holders,)),
            pltpu.SemaphoreType.DMA((share,)),
        ],
        compiler_params=pltpu.CompilerParams(collective_id=0, has_side_effects=True),
        name="gather_designs",
    )(own)


def factor_block(work):
    row_iota = lax.broadcasted_iota(jnp.int32, (GROUP, BLOCK), 0)
    for first in range(0, BLOCK, GROUP):
        rows = work[first : first + GROUP, :]
        left, right = rows[:, :BLOCK], rows[:, BLOCK:]
        columns = [
            jnp.broadcast_to(left[:, first + k : first + k + 1], (GROUP, BLOCK))
            for k in range(GROUP)
        ]
        scales = jnp.zeros((GROUP, BLOCK), F32)
        for k in range(GROUP):
            root = lax.rsqrt(columns[k][k : k + 1, :])
            inverse = root * root
            scales = jnp.where(row_iota == k, root, scales)
            below = jnp.where(row_iota > k, columns[k], 0.0)
            for m in range(k + 1, GROUP):
                columns[m] = columns[m] - (below * columns[m][k : k + 1, :]) * inverse
            left = left - below * (left[k : k + 1, :] * inverse)
            right = right - below * (right[k : k + 1, :] * inverse)
        left, right = left * scales, right * scales
        work[first : first + GROUP, :BLOCK] = left
        work[first : first + GROUP, BLOCK:] = right
        last = first + GROUP
        if last < BLOCK:
            high, mid, low = split3(jnp.concatenate([left, right], 1))
            a = jnp.concatenate([high, high, mid, high, mid, low], 0)[:, :BLOCK]
            b = jnp.concatenate([high, mid, high, low, mid, high], 0)
            work[last:, :] = work[last:, :] - dot_tn(a, b)[last:, :]


def factor_kernel(panel, root_weights, inverse, factor, matrix, upper, work):
    width = factor.shape[1]
    scaled = panel[...] * root_weights[...]
    flipped = scaled.T
    inner = dot_tn(scaled, scaled, HIGHEST)
    squares = jnp.sum(scaled * scaled, axis=0, keepdims=True)
    squares_col = jnp.sum(flipped * flipped, axis=1, keepdims=True)
    kernel = signal_variance * jnp.exp(-(squares_col + squares - 2.0 * inner))
    gap = flipped[:, -2:-1] - scaled[-2:-1, :]
    row_iota = lax.broadcasted_iota(jnp.int32, (PANEL, PANEL), 0)
    col_iota = lax.broadcasted_iota(jnp.int32, (PANEL, PANEL), 1)
    matrix[...] = kernel * (1.0 - 2.0 * gap * gap) + jnp.where(
        row_iota == col_iota, nugget_level, 0.0
    )
    upper[...] = jnp.zeros_like(upper)
    work_row = lax.broadcasted_iota(jnp.int32, (BLOCK, BLOCK), 0)
    work_col = lax.broadcasted_iota(jnp.int32, (BLOCK, BLOCK), 1)
    identity = jnp.where(work_row == work_col, 1.0, 0.0)
    blocks = PANEL // BLOCK

    @pl.loop(0, blocks)
    def _(at):
        offset = pl.multiple_of(at * BLOCK, BLOCK)
        work[:, :BLOCK] = matrix[pl.ds(offset, BLOCK), pl.ds(offset, BLOCK)]
        work[:, BLOCK:] = identity
        factor_block(work)
        part_upper = jnp.where(work_col >= work_row, work[:, :BLOCK], 0.0)
        part_inverse = jnp.where(work_col <= work_row, work[:, BLOCK:], 0.0)
        for k in range(blocks):

            @pl.when(at == k)
            def _():
                low, high = k * BLOCK, (k + 1) * BLOCK
                solved = jnp.dot(
                    part_inverse,
                    matrix[low:high, :],
                    precision=HIGHEST,
                    preferred_element_type=F32,
                )
                pieces = [part_inverse]
                if k > 0:
                    pieces.insert(0, solved[:, :low])
                if high < PANEL:
                    pieces.append(solved[:, high:])
                    upper[low:high, high:] = solved[:, high:]
                upper[low:high, low:high] = part_upper
                whole = jnp.concatenate(pieces, 1)
                matrix[low:high, :] = whole
                if high < PANEL:
                    matrix[high:, low:high] = jnp.zeros((PANEL - high, BLOCK), F32)
                    matrix[high:, :] = matrix[high:, :] - dot_tn(
                        solved[:, high:], whole, HIGHEST
                    )

    inverse[...] = jnp.where(col_iota <= row_iota, matrix[...], 0.0)
    col = lax.axis_index("pcol")
    first = pl.multiple_of(col * width, width)
    factor[...] = upper[pl.ds(first, width), :].T


def factor_panel(panel, root_weights, width):
    return pl.pallas_call(
        factor_kernel,
        out_shape=(
            jax.ShapeDtypeStruct((PANEL, PANEL), F32),
            jax.ShapeDtypeStruct((PANEL, width), F32),
        ),
        in_specs=[pl.BlockSpec(memory_space=pltpu.VMEM)] * 2,
        out_specs=(pl.BlockSpec(memory_space=pltpu.VMEM), pl.BlockSpec(memory_space=pltpu.VMEM)),
        scratch_shapes=[
            pltpu.VMEM((PANEL, PANEL), F32),
            pltpu.VMEM((PANEL, PANEL), F32),
            pltpu.VMEM((BLOCK, 2 * BLOCK), F32),
        ],
        compiler_params=pltpu.CompilerParams(vmem_limit_bytes=32 * 2**20),
        name="factor_panel",
    )(panel, root_weights)


CHUNK = 128


def update_kernel(
    rows, cols, panel, weights_row, weights_col, inverse, trailing,
    updated, shard,
    panel_parts, panel_rows, inverse_parts, cross, row_parts, col_parts,
):
    i, j = pl.program_id(0), pl.program_id(1)
    width = shard.shape[1]
    tile_m, tile_n = trailing.shape
    half = PANEL // 2

    @pl.when((i == 0) & (j == 0))
    def _():
        scaled = panel[...] * weights_col[...]
        high, mid = split2(scaled)
        panel_parts[...] = jnp.concatenate([high, mid, high, mid], 0)
        panel_rows[0:1, :] = jnp.sum(scaled * scaled, axis=0, keepdims=True)
        panel_rows[1:2, :] = scaled[-2:-1, :]
        panel_rows[2:3, :] = scaled[-1:, :]
        high, low = split2(inverse[...])
        inverse_parts[...] = jnp.concatenate([high, low, high], 1)

    def factor_rows(points):
        scaled = points * weights_row[...]
        high, mid = split2(scaled)
        parts = jnp.concatenate([high, high, mid, mid], 1)
        inner = jnp.dot(parts, panel_parts[...], preferred_element_type=F32)
        squares = jnp.sum(scaled * scaled, axis=1, keepdims=True)
        kernel = jnp.exp(2.0 * inner - squares - panel_rows[0:1, :])
        value = (signal_variance * math.sqrt(2.0)) * kernel * (
            scaled[:, -2:-1] - panel_rows[1:2, :]
        )
        derivative = value * (math.sqrt(2.0) * (panel_rows[2:3, :] - scaled[:, -1:]))
        for lane in range(0, PANEL, 128):
            tile = cross.at[lane // 128]
            tile[pl.ds(0, CHUNK, stride=2), :] = derivative[:, lane : lane + 128]
            tile[pl.ds(1, CHUNK, stride=2), :] = value[:, lane : lane + 128]
        high, low = split2(jnp.concatenate([cross[at] for at in range(PANEL // 128)], 1))
        parts = jnp.concatenate([high, high, low], 1)
        left = jnp.concatenate([high[:, :half], high[:, :half], low[:, :half]], 1)
        left_inverse = jnp.concatenate(
            [inverse_parts[:half, part * PANEL : part * PANEL + half] for part in range(3)], 1
        )
        solved = jnp.concatenate(
            [dot_nt(left, left_inverse), dot_nt(parts, inverse_parts[half:, :])], 1
        )
        return parts, solved

    @pl.when(j == 0)
    def _():
        col = lax.axis_index("pcol")
        first = pl.multiple_of(col * width, width)

        @pl.loop(0, tile_m // (2 * CHUNK))
        def _(at):
            start = pl.multiple_of(at * CHUNK, CHUNK)
            parts, solved = factor_rows(rows[pl.ds(start, CHUNK), :])
            high, low = split2(solved)
            place = pl.ds(pl.multiple_of(at * 2 * CHUNK, 2 * CHUNK), 2 * CHUNK)
            row_parts[place, :] = jnp.concatenate([high, high, low], 1)
            shard[place, :] = dot_nt(parts, inverse_parts[pl.ds(first, width), :])

    @pl.when(i == 0)
    def _():
        @pl.loop(0, tile_n // (2 * CHUNK))
        def _(at):
            start = pl.multiple_of(at * CHUNK, CHUNK)
            _, solved = factor_rows(cols[pl.ds(start, CHUNK), :])
            high, low = split2(solved)
            place = pl.ds(pl.multiple_of(j * tile_n + at * 2 * CHUNK, 2 * CHUNK), 2 * CHUNK)
            col_parts[place, :] = jnp.concatenate([high, low, high], 1)

    @pl.loop(0, tile_n // 256)
    def _(at):
        lanes = pl.ds(pl.multiple_of(at * 256, 256), 256)
        place = pl.ds(pl.multiple_of(j * tile_n + at * 256, 256), 256)
        updated[:, lanes] = trailing[:, lanes] - dot_nt(row_parts[...], col_parts[place, :])


def update(designs, cols, panel, root_weights, inverse, trailing, width):
    height, extent = trailing.shape
    tile_m, tile_n = min(1024, height), min(1024, extent)
    variables = designs.shape[1]
    return pl.pallas_call(
        update_kernel,
        grid=(height // tile_m, extent // tile_n),
        out_shape=(
            jax.ShapeDtypeStruct((height, extent), F32),
            jax.ShapeDtypeStruct((height, width), F32),
        ),
        in_specs=[
            pl.BlockSpec((tile_m // 2, variables), lambda i, j: (i, 0)),
            pl.BlockSpec((tile_n // 2, variables), lambda i, j: (j, 0)),
            pl.BlockSpec((variables, PANEL), lambda i, j: (0, 0)),
            pl.BlockSpec((1, variables), lambda i, j: (0, 0)),
            pl.BlockSpec((variables, 1), lambda i, j: (0, 0)),
            pl.BlockSpec((PANEL, PANEL), lambda i, j: (0, 0)),
            pl.BlockSpec((tile_m, tile_n), lambda i, j: (i, j)),
        ],
        out_specs=(
            pl.BlockSpec((tile_m, tile_n), lambda i, j: (i, j)),
            pl.BlockSpec((tile_m, width), lambda i, j: (i, 0)),
        ),
        scratch_shapes=[
            pltpu.VMEM((4 * variables, PANEL), BF16),
            pltpu.VMEM((8, PANEL), F32),
            pltpu.VMEM((PANEL, 3 * PANEL), BF16),
            pltpu.VMEM((PANEL // 128, 2 * CHUNK, 128), F32),
            pltpu.VMEM((tile_m, 3 * PANEL), BF16),
            pltpu.VMEM((extent, 3 * PANEL), BF16),
        ],
        compiler_params=pltpu.CompilerParams(vmem_limit_bytes=56 * 2**20),
        name="update_trailing",
    )(designs, cols, panel, root_weights[None, :], root_weights[:, None], inverse, trailing)


def body(designs, length_weights, trailing):
    grid_rows = lax.axis_size("prow")
    grid_cols = lax.axis_size("pcol")
    width = PANEL // grid_cols
    root_weights = jnp.sqrt(length_weights)
    panel, cols = gather_designs(designs.T, grid_rows, grid_cols)
    inverse, factor = factor_panel(panel, root_weights[:, None], width)
    updated, shard = update(designs, cols.T, panel, root_weights, inverse, trailing, width)
    return updated, shard, factor


def solution(mesh):
    in_specs = (P("prow", None), P(), P("prow", "pcol"))
    out_specs = (P("prow", "pcol"), P("prow", "pcol"), P(None, "pcol"))
    return jax.shard_map(body, mesh=mesh, in_specs=in_specs, out_specs=out_specs, check_vma=False)
```

time: 687 us -> 120 us (0.17)
  the two profiles are of different devices: /device:TPU:19 before, /device:TPU:29 now
where the time goes in v1:
time: 120 us
  Pallas kernels  111 us (92%)
  local copies, waits for them, and re-layouts  7.53 us (6%)
    pallas_call x1, Pallas kernels, update(): pl.pallas_call(update_kernel, grid=(height // tile_m, extent // tile_n),...  58.3 us
    pallas_call x1, Pallas kernels, gather_designs(): pl.pallas_call(functools.partial(gather_kernel, grid_rows, grid_cols), ou...  33.1 us
    pallas_call x1, Pallas kernels, factor_panel(): pl.pallas_call(factor_kernel, out_shape=(jax.ShapeDtypeStruct((PANEL, PAN...  19.9 us
    unnamed x7, local copies, waits for them, and re-layouts  3.91 us

profile of v1, /device:TPU:29, one launch (start us, length us, event | category | flops | bytes accessed | tf_op | source)
XLA Modules:
  0.0 119.5 jit_solution(6111408998564778054)
XLA Ops:
  0.6 1.2 sqrt_bitcast_fusion
  1.8 0.1 copy.9.root_weights.weights_col
  1.9 0.0 copy-start.2
  1.9 2.0 %copy.8.rows = f32[1024,64]{1,0:T(8,128)} copy(f32[1024,64]{0,1:T(8,128)} %param.3) | data formatting | bytes 524288 | tf_op args[0]
  3.9 33.1 %gather_designs.1 = (f32[64,512]{1,0:T(8,128)}, f32[64,2048]{1,0:T(8,128)}) custom-call(f32[64,1024]{1,0:T(8,128)} %bitcast.7), custom_call_target="tpu_custom_call" | custom-call | tf_op jit(solution)/shard_map/gather_designs/pallas_call | solution.py:106
  37.0 2.4 %copy.6 = f32[64,2048]{0,1:T(8,128)} copy(f32[64,2048]{1,0:T(8,128)} %get-tuple-element.9) | data formatting | bytes 1048576 | tf_op jit(solution)/shard_map/gather_designs/pallas_call | solution.py:106
  39.4 0.0 copy-start.1
  39.4 0.9 copy-done.1
  40.3 19.9 %factor_panel.1 = (f32[512,512]{1,0:T(8,128)S(1)}, f32[512,128]{1,0:T(8,128)}) custom-call(f32[64,512]{1,0:T(8,128)S(1)} %copy-done.1, f32[64,1]{1,0:T(8,128)S(1)} %copy.9.root_weights.weights_col), custom_call_target="tpu_custom_call" | custom-call | tf_op jit(solution)/shard_map/factor_panel/pallas_call | solution.py:216
  60.1 0.0 copy-start
  60.1 1.0 copy-done
  61.2 0.0 copy-done.2
  61.2 58.3 %update_trailing.1 = (f32[2048,4096]{1,0:T(8,128)}, f32[2048,128]{1,0:T(8,128)}) custom-call(f32[1024,64]{1,0:T(8,128)} %copy.8.rows, f32[2048,64]{1,0:T(8,128)} %bitcast.6, f32[64,512]{1,0:T(8,128)} %get-tuple-element.10.panel, f32[1,64]{1,0:T(1,128)} %get-tuple-element.16.weights_row, f32[64,1]{1,0:T(8,128)} %copy-done.2, f32[512,512]{1,0:T(8,128)} %copy-done, ...), custom_call_target="tpu_custom_call" | custom-call | tf_op jit(solution)/shard_map/update_trailing/pallas_call | solution.py:319
Async XLA Ops:
  1.9 59.3 %copy-start.2 = (f32[64,1]{1,0:T(8,128)}, f32[64,1]{1,0:T(8,128)S(1)}, u32[]{:S(2)}) copy-start(f32[64,1]{1,0:T(8,128)S(1)} %copy.9.root_weights.weights_col) | copy-start | bytes 772
  39.4 0.9 copy-start.1
  60.1 1.0 copy-start
